TPU v7x, 32 devices: a whole 2x2x4 slice. The times are simulated.
32 devices in a mesh: mol: 16 (over z, x, core), tp: 2 (over y).
Axes of the slice: x: 2, y: 2, z: 4, core: 2. Of those that a mesh axis runs over, the one named last changes fastest.
Arguments:
- hidden_in: bfloat16 [16384, 768], P(('mol', 'tp')), may hold values from -6 to 6
- positions: float32 [3, 16384], P(None, ('mol', 'tp')), may hold values from -8 to 8
- atom_types: int32 [16384], P(('mol', 'tp')), may hold values from 0 to 15
- hop_counts: int32 [16384, 64], P(('mol', 'tp')), may hold values from 0 to 15
- edge_types: int32 [16384, 64], P(('mol', 'tp')), may hold values from 0 to 7
- lengths: int32 [256], P('mol'), may hold values from 20 to 60
- branches: int32 [256, 2], P(('mol', 'tp')), may hold values from 0 to 1, as said below
- attn_gain: float32 [768], replicated, may hold values from 0.5 to 1.5
- attn_shift: float32 [768], replicated, may hold values from -1.75 to 1.75
- qkv_weight: bfloat16 [768, 3, 768], P(None, None, 'tp'), may hold values from -0.21875 to 0.21875
- proj_weight: bfloat16 [768, 768], P('tp'), may hold values from -0.875 to 0.875
- ffn_gain: float32 [768], replicated, may hold values from 0.5 to 1.5
- ffn_shift: float32 [768], replicated, may hold values from -1.75 to 1.75
- up_weight: bfloat16 [768, 768], P(None, 'tp'), may hold values from -0.21875 to 0.21875
- up_bias: float32 [768], replicated, may hold values from -3 to 3
- down_weight: bfloat16 [768, 768], P('tp'), may hold values from -0.21875 to 0.21875
- down_bias: float32 [768], replicated, may hold values from -1.75 to 1.75
- kernel_scale: float32 [16, 16], replicated, may hold values from 0.5 to 1.5
- kernel_shift: float32 [16, 16], replicated, may hold values from -3 to 3
- centers: float32 [128], replicated, may hold values from 0 to 6
- spreads: float32 [128], replicated, may hold values from 0.5 to 2
- first_weight: bfloat16 [128, 128], replicated, may hold values from -1.5 to 1.5
- first_bias: float32 [128], replicated, may hold values from -3 to 3
- second_weight: bfloat16 [128, 32], replicated, may hold values from -0.75 to 0.75
- hop_table: float32 [16, 32], replicated, may hold values from -3 to 3
- edge_table: float32 [8, 32], replicated, may hold values from -3 to 3
- cotangent: bfloat16 [16384, 768], P(('mol', 'tp')), may hold values from -6 to 6
Outputs:
- output: bfloat16 [16384, 768], P(('mol', 'tp'))
- grad_input: bfloat16 [16384, 768], P(('mol', 'tp'))
- grad_attn_gain: float32 [768], replicated
- grad_attn_shift: float32 [768], replicated
- grad_qkv_weight: float32 [768, 3, 768], P(None, None, 'tp')
- grad_proj_weight: float32 [768, 768], P('tp')
- grad_ffn_gain: float32 [768], replicated
- grad_ffn_shift: float32 [768], replicated
- grad_up_weight: float32 [768, 768], P(None, 'tp')
- grad_up_bias: float32 [768], replicated
- grad_down_weight: float32 [768, 768], P('tp')
- grad_down_bias: float32 [768], replicated
- grad_kernel_scale: float32 [16, 16], replicated
- grad_kernel_shift: float32 [16, 16], replicated
- grad_centers: float32 [128], replicated
- grad_spreads: float32 [128], replicated
- grad_first_weight: float32 [128, 128], replicated
- grad_first_bias: float32 [128], replicated
- grad_second_weight: float32 [128, 32], replicated
- grad_hop_table: float32 [16, 32], replicated
- grad_edge_table: float32 [8, 32], replicated
Inputs may be any that keep to these rules, and one draw needn't show every extreme that they name: The molecule of slot s occupies its first lengths[s] atom positions; the other positions of the slot are padding and are never attended to. `branches`: column 0 is a molecule's 2D flag and column 1 its 3D flag; every row has at least one set, and 2D-only, 3D-only and joint molecules all occur.
All inputs are finite; a program needn't handle non-finite values.
Results may differ from a plain program's by a relative error of at most 0.025.
Values may be sent and summed in bfloat16 or wider, within the bound.
A program may use at most 192 MiB of HBM per device.

v0:
```python
import functools
from types import SimpleNamespace

import jax
import jax.numpy as jnp
from jax import lax
from jax.experimental import pallas as pl
from jax.experimental.pallas import tpu as pltpu
from jax.sharding import PartitionSpec as P

D = 768
H = 32
HD = 24
FF = 768
K = 128
SLOT = 64
HALF = SLOT // 2
HALF_D = D // 2
PAIRS = SLOT * SLOT
HOPS = 16
EDGES = 8
ATOMS = 16
GROUP = 4
GROUPS = H // GROUP
HOT = 32

highest = lax.Precision.HIGHEST
neg_large = -1e30
root_tau = 2.5066282746310002
root_half = 0.7071067811865476
inv_root_tau = 0.3989422804014327
head_scale = HD ** (-0.5)
VMEM_BYTES = 62 * 1024 * 1024
TILE = 512

SECOND_ROWS = K
TABLE_ROWS = SECOND_ROWS + H
KERNEL_ROWS = TABLE_ROWS + H
VECTOR_ROWS = KERNEL_ROWS + 8
SMALL_ROWS = 256

MESH = pl.DeviceIdType.MESH
f32 = jnp.float32
bf16 = jnp.bfloat16


def dot_nn(left, right, precision=None):
    return lax.dot_general(left, right, (((1,), (0,)), ((), ())), precision=precision, preferred_element_type=f32)


def dot_nt(left, right, precision=None):
    return lax.dot_general(left, right, (((1,), (1,)), ((), ())), precision=precision, preferred_element_type=f32)


def dot_tn(left, right, precision=None):
    return lax.dot_general(left, right, (((0,), (0,)), ((), ())), precision=precision, preferred_element_type=f32)


def iota(shape, dim):
    return lax.broadcasted_iota(jnp.int32, shape, dim)


def gelu_parts(values):
    size = jnp.abs(values)
    bell = jnp.exp(values * values * -0.5)
    denominator = 1.0 + (0.3275911 * root_half) * size
    t = pl.reciprocal(denominator, approx=True)
    series = 0.5 * 1.061405429
    for factor in (-1.453152027, 1.421413741, -0.284496736, 0.254829592):
        series = series * t + 0.5 * factor
    tail = series * t * bell
    gelu = jnp.maximum(values, 0.0) - size * tail
    outer = tail - size * (bell * inv_root_tau)
    return gelu, jnp.where(values >= 0.0, 1.0 - outer, outer)


def gelu_pair(values):
    size = jnp.abs(values)
    bell = jnp.exp(values * values * -0.5)
    t = pl.reciprocal(1.0 + (0.3275911 * root_half) * size, approx=True)
    series = 0.5 * 1.061405429
    for factor in (-1.453152027, 1.421413741, -0.284496736, 0.254829592):
        series = series * t + 0.5 * factor
    tail = (series * t * bell).astype(bf16)
    density = (bell * inv_root_tau).astype(bf16)
    values = values.astype(bf16)
    size = jnp.abs(values)
    outer = tail - size * density
    one, zero = jnp.ones((), bf16), jnp.zeros((), bf16)
    return jnp.maximum(values, zero) - size * tail, jnp.where(values >= zero, one - outer, outer)


def to_column(row):
    size = row.shape[1]
    same = iota((size, size), 0) == iota((size, size), 1)
    return jnp.sum(jnp.where(same, row, 0.0), axis=1, keepdims=True)


def half_swap(values):
    return pltpu.roll(values, 64, 1)


def low_lanes(rows):
    return iota((rows, 128), 1) < 64


def vmem(count):
    return [pl.BlockSpec(memory_space=pltpu.VMEM)] * count


def row_of(ref):
    return ref[...].reshape(1, ref.shape[0])


def place():
    mol = lax.axis_index("mol")
    return mol % 2, (mol // 2) % 2, mol // 4, lax.axis_index("tp")


def greet(peers):
    for peer in peers:
        pl.semaphore_signal(pltpu.get_barrier_semaphore(), inc=1, device_id=peer, device_id_type=MESH)


def await_greetings(peers):
    pl.semaphore_wait(pltpu.get_barrier_semaphore(), len(peers))


def window(group):
    first = GROUP * HD * group
    start = first // 128 * 128
    width = 128 if first - start + GROUP * HD <= 128 else 256
    return start, width, first - start


def head_masks(group, kind):
    _, width, offset = window(group)
    lane = iota((1, width), 1)
    return [
        ((lane >= offset + HD * h) & (lane < offset + HD * (h + 1))).astype(f32).astype(kind) for h in range(GROUP)
    ]


def spread_heads(values, group):
    return jnp.concatenate([values * mask for mask in head_masks(group, bf16)], axis=0)


def gather_heads(values, group):
    masks = head_masks(group, f32)
    total = values[:SLOT] * masks[0]
    for h in range(1, GROUP):
        total = total + values[SLOT * h : SLOT * (h + 1)] * masks[h]
    return total


def standardize(values):
    centred = values - jnp.mean(values, axis=-1, keepdims=True)
    inv_std = lax.rsqrt(jnp.mean(centred * centred, axis=-1, keepdims=True) + 1e-05)
    return centred * inv_std, inv_std


def norm_back(d_normed, scaled, inv_std, gain):
    weighted = d_normed * gain
    inner_a = jnp.mean(weighted, axis=-1, keepdims=True)
    inner_b = jnp.mean(weighted * scaled, axis=-1, keepdims=True)
    return inv_std * (weighted - inner_a - scaled * inner_b)


def column_sum(values):
    return jnp.sum(values, axis=0, keepdims=True)


class Peers:
    def __init__(self):
        self.core, self.x, self.z, self.tp = place()
        mol = lax.axis_index("mol")
        self.over_core = {"mol": mol + 1 - 2 * self.core}
        self.over_x = {"mol": mol + 2 - 4 * self.x}
        self.over_tp = {"tp": 1 - self.tp}
        self.turn = [lax.rem(self.z + d, 4) for d in range(4)]
        self.over_z = [{"mol": self.turn[d] * 4 + self.x * 2 + self.core} for d in range(4)]

    def neighbour(self, k):
        core = self.core + (1 - 2 * self.core) * (k & 1)
        x = self.x + (1 - 2 * self.x) * (k >> 1 & 1)
        tp = self.tp + (1 - 2 * self.tp) * (k >> 2)
        return core * 4 + tp * 2 + x, {"mol": self.z * 4 + x * 2 + core, "tp": tp}

    def everyone(self):
        return [self.neighbour(k)[1] for k in range(1, 8)] + self.over_z[1:]


def span(start, size):
    return pl.ds(pl.multiple_of(start, size), size)


def add_rows(target, source, rows):
    step = 96 if rows % 96 == 0 else min(rows, 32)

    def piece(i, _):
        at = pl.ds(pl.multiple_of(i * step, step), step)
        target[at, :] = target[at, :] + source[at, :]
        return 0

    lax.fori_loop(0, rows // step, piece, 0)


class Reduction:
    kinds = 11

    def __init__(self, peers, part, total, from_core, from_tp, from_x, from_z, sends, recvs):
        self.peers, self.part, self.total = peers, part, total
        self.from_core, self.from_tp, self.from_x, self.from_z = from_core, from_tp, from_x, from_z
        self.sends, self.recvs = sends, recvs
        self.half = from_core.shape[2]
        self.quarter, self.least = self.half // 2, self.half // 8

    def rows(self, b, level):
        p = self.peers
        at = b * 2 * self.half + p.core * self.half
        if level > 0:
            at = at + p.x * self.quarter
        return at + p.z * self.least if level > 1 else at

    def copy(self, b, kind):
        p = self.peers
        part, total = self.part, self.total
        half, quarter, least = self.half, self.quarter, self.least
        if kind == 0:
            src = part.at[:, span(b * 2 * half + (1 - p.core) * half, half)]
            dst, peer = self.from_core.at[b], p.over_core
        elif kind == 1:
            src, dst, peer = part.at[1 - p.tp, span(self.rows(b, 0), half)], self.from_tp.at[b], p.over_tp
        elif kind == 2:
            src = part.at[p.tp, span(self.rows(b, 0) + (1 - p.x) * quarter, quarter)]
            dst, peer = self.from_x.at[b], p.over_x
        elif kind < 6:
            d = kind - 2
            src = part.at[p.tp, span(self.rows(b, 1) + p.turn[d] * least, least)]
            dst, peer = self.from_z.at[b, d - 1], p.over_z[d]
        elif kind < 9:
            src = dst = total.at[span(self.rows(b, 2), least)]
            peer = p.over_z[kind - 5]
        elif kind == 9:
            src = dst = total.at[span(self.rows(b, 1), quarter)]
            peer = p.over_x
        else:
            src = dst = total.at[span(self.rows(b, 0), half)]
            peer = p.over_core
        return pltpu.make_async_remote_copy(
            src_ref=src, dst_ref=dst, send_sem=self.sends.at[b, kind], recv_sem=self.recvs.at[b, kind],
            device_id=peer, device_id_type=MESH,
        )

    def act(self, b, stage):
        p = self.peers
        half, quarter, least = self.half, self.quarter, self.least
        part = self.part
        if stage == 0:
            self.copy(b, 0).start()
        elif stage == 1:
            self.copy(b, 0).wait_recv()
            at = span(self.rows(b, 0), half)
            add_rows(part.at[1 - p.tp, at], self.from_core.at[b, 1 - p.tp], half)
            self.copy(b, 1).start()
            add_rows(part.at[p.tp, at], self.from_core.at[b, p.tp], half)
        elif stage == 2:
            self.copy(b, 1).wait_recv()
            away, mine = (1 - p.x) * quarter, p.x * quarter
            at = self.rows(b, 0)
            add_rows(part.at[p.tp, span(at + away, quarter)], self.from_tp.at[b, span(away, quarter)], quarter)
            self.copy(b, 2).start()
            add_rows(part.at[p.tp, span(at + mine, quarter)], self.from_tp.at[b, span(mine, quarter)], quarter)
        elif stage == 3:
            self.copy(b, 2).wait_recv()
            add_rows(part.at[p.tp, span(self.rows(b, 1), quarter)], self.from_x.at[b], quarter)
            for kind in (3, 4, 5):
                self.copy(b, kind).start()
        elif stage == 4:
            for kind in (3, 4, 5):
                self.copy(b, kind).wait_recv()
            mine = span(self.rows(b, 2), least)
            value = part[p.tp, mine, :].astype(f32)
            for d in range(3):
                value = value + self.from_z[b, d].astype(f32)
            self.total[mine, :] = value.astype(bf16)
            for kind in (6, 7, 8):
                self.copy(b, kind).start()
        elif stage == 5:
            for kind in (6, 7, 8):
                self.copy(b, kind).wait_recv()
            self.copy(b, 9).start()
        elif stage == 6:
            self.copy(b, 9).wait_recv()
            self.copy(b, 10).start()
        elif stage == 7:
            self.copy(b, 10).wait_recv()
        else:
            for kind in range(self.kinds):
                self.copy(b, kind).wait_send()


class SmallReduction:
    def __init__(self, peers, part, total, from_near, from_z, sends, recvs):
        self.peers, self.part, self.total, self.from_near, self.from_z = peers, part, total, from_near, from_z
        self.sends, self.recvs = sends, recvs
        p = peers
        self.near = [p.neighbour(k) for k in range(8)]
        self.mine = span(self.near[0][0] * 32, 32)

    def copy(self, kind):
        p = self.peers
        if kind < 7:
            index, peer = self.near[kind + 1]
            src, dst = self.part.at[span(index * 32, 32)], self.from_near.at[kind]
        elif kind < 10:
            src = dst = self.from_z.at[p.z]
            peer = p.over_z[kind - 6]
        else:
            src = dst = self.total.at[self.mine]
            peer = self.near[kind - 9][1]
        return pltpu.make_async_remote_copy(
            src_ref=src, dst_ref=dst, send_sem=self.sends.at[kind], recv_sem=self.recvs.at[kind],
            device_id=peer, device_id_type=MESH,
        )

    def act(self, stage):
        hops = (range(0, 7), range(7, 10), range(10, 17))
        if stage == 4:
            for kind in range(17):
                self.copy(kind).wait_send()
            return
        if stage > 0:
            for kind in hops[stage - 1]:
                self.copy(kind).wait_recv()
        if stage == 1:
            value = self.part[self.mine, :]
            for k in range(7):
                value = value + self.from_near[k]
            self.from_z[self.peers.z] = value
        elif stage == 2:
            self.total[self.mine, :] = (self.from_z[0] + self.from_z[1]) + (self.from_z[2] + self.from_z[3])
        if stage < 3:
            for kind in hops[stage]:
                self.copy(kind).start()


def big_scratch(rows, lanes):
    half = rows // 2
    sems = pltpu.SemaphoreType.DMA((3, Reduction.kinds))
    return [
        pltpu.VMEM((3, 2, half, lanes), bf16), pltpu.VMEM((3, half, lanes), bf16),
        pltpu.VMEM((3, half // 2, lanes), bf16), pltpu.VMEM((3, 3, half // 8, lanes), bf16), sems, sems,
    ]


def small_scratch():
    return [
        pltpu.VMEM((7, 32, 128), f32), pltpu.VMEM((4, 32, 128), f32),
        pltpu.SemaphoreType.DMA((17,)), pltpu.SemaphoreType.DMA((17,)),
    ]


class Gather:
    pieces = 6

    def __init__(self, peers, whole, sends, recvs):
        self.peers, self.whole, self.sends, self.recvs = peers, whole, sends, recvs
        self.quarter = peers.x * 2 + peers.core
        self.next_quarter = (1 - peers.x) * 2 + peers.core

    def rows(self, ref, quarter):
        count = ref.shape[0] // 4
        return ref.at[span(quarter * count, count), :]

    def copy(self, index, kind):
        p = self.peers
        if kind == 0:
            src = dst = self.rows(self.whole(index, p.tp), self.quarter)
            peer = p.over_tp
        elif kind == 1:
            src = dst = self.rows(self.whole(index, 1 - p.tp), self.quarter)
            peer = p.over_x
        else:
            src = dst = self.rows(self.whole(index, 1 - p.tp), self.quarter if kind == 2 else self.next_quarter)
            peer = p.over_core
        return pltpu.make_async_remote_copy(
            src_ref=src, dst_ref=dst, send_sem=self.sends.at[index, kind], recv_sem=self.recvs.at[index, kind],
            device_id=peer, device_id_type=MESH,
        )

    def start(self, indices):
        for index in indices:
            self.copy(index, 0).start()

    def onward_x(self, index):
        self.copy(index, 0).wait_recv()
        self.copy(index, 1).start()
        self.copy(index, 2).start()

    def onward_core(self, index):
        self.copy(index, 1).wait_recv()
        self.copy(index, 3).start()

    def arrive(self, index):
        self.copy(index, 2).wait_recv()
        self.copy(index, 3).wait_recv()

    def finish(self):
        for index in range(self.pieces):
            for kind in range(4):
                self.copy(index, kind).wait_send()


def square_turn(values):
    rows, lanes = values.shape
    if lanes < 128:
        values = jnp.concatenate([values, jnp.zeros((rows, 128 - lanes), f32)], axis=1)
    if rows < 128:
        values = jnp.concatenate([values, jnp.zeros((128 - rows, 128), f32)], axis=0)
    return values.T


def widen(values):
    return jnp.concatenate([values] * (TILE // 128), axis=1)


def strips():
    return [slice(16 * i, 16 * (i + 1)) for i in range(K // 16)]


def four_rows(ref, slot, first):
    return jnp.concatenate([ref[slot, pl.ds(first + i, 1), :] for i in range(TILE // 128)], axis=1)


def hot_rows(values, count):
    return (values == iota((count, TILE), 0).astype(f32)).astype(f32)


def fold_lanes(values):
    total = values[:, :128]
    for i in range(1, TILE // 128):
        total = total + values[:, 128 * i : 128 * (i + 1)]
    return total


def twice(ref, values):
    none = jnp.zeros_like(values)
    ref[...] = jnp.concatenate(
        [jnp.concatenate([values, none], axis=1), jnp.concatenate([none, values], axis=1)], axis=0
    ).astype(bf16)


def dot_halves(weights, pieces):
    values = jnp.concatenate(pieces, axis=0)
    half = TILE // 2
    both = dot_nn(weights, jnp.concatenate([values[:, :half], values[:, half:]], axis=0))
    rows = both.shape[0] // 2
    return jnp.concatenate([both[:rows], both[rows:]], axis=1)


def prepare_pairs(r):
    spr = to_column(row_of(r.spreads))
    r.cols[0] = jnp.broadcast_to(to_column(row_of(r.centers)), (K, 128))
    r.cols[1] = jnp.broadcast_to(root_half / spr, (K, 128))
    r.cols[2] = jnp.broadcast_to(-jnp.log(root_tau * spr), (K, 128))
    r.cols[3] = jnp.broadcast_to(to_column(row_of(r.first_bias)), (K, 128))
    r.cols[4] = jnp.broadcast_to(1.0 / spr, (K, 128))
    twice(r.w1, r.first_weight[...].astype(f32))
    twice(r.w1t, r.first_weight[...].astype(f32).T)
    r.w2[...] = square_turn(r.second_weight[...].astype(f32))
    table = jnp.concatenate([r.hop_table[...], r.edge_table[...], jnp.zeros((128 - HOPS - EDGES, H), f32)], axis=0)
    table = jnp.concatenate([table, jnp.zeros((128, 128 - H), f32)], axis=1).T[:H, :HOT]
    one = table.astype(bf16).astype(f32)
    r.base[...] = jnp.concatenate(
        [r.second_weight[...].astype(f32), one, table - one, jnp.zeros((H, 64), f32)], axis=1
    )


def bf16_parts(values, count):
    parts = []
    for _ in range(count):
        parts.append(values.astype(bf16))
        values = values - parts[-1].astype(f32)
    return parts


def pair_tables(r, slots):
    low = low_lanes(HALF)
    low_row = low_lanes(1)
    tables = [part.astype(f32) for ref in (r.kernel_scale, r.kernel_shift) for part in bf16_parts(ref[...], 3)]
    tables = jnp.concatenate([square_turn(part)[:ATOMS, :ATOMS] for part in tables], axis=1)
    tables = jnp.concatenate([tables, jnp.zeros((ATOMS, 128 - 6 * ATOMS), f32)], axis=1).astype(bf16)
    for group in range(slots // 2):
        lanes = slice(128 * group, 128 * (group + 1))
        atoms = r.atoms[lanes].astype(f32).reshape(1, 128)
        rows = jnp.concatenate([r.positions[:, lanes], atoms, jnp.zeros((4, 128), f32)], axis=0)
        columns = square_turn(rows)
        key_hot = (columns[:, 3:4] == iota((128, ATOMS), 1).astype(f32)).astype(f32).astype(bf16)
        picks = dot_nn(key_hot, tables).astype(bf16)
        turned = half_swap(rows)
        for s in range(2):
            slot = 2 * group + s
            tokens = slice(SLOT * s, SLOT * (s + 1))
            double = jnp.where(low_lanes(8), *((rows, turned) if s == 0 else (turned, rows)))
            total = None
            for c in range(3):
                column = columns[tokens, c : c + 1]
                offset = jnp.where(low, column[:HALF], column[HALF:]) - double[c : c + 1]
                total = offset * offset if total is None else total + offset * offset
            distance = jnp.sqrt(total)
            query_hot = (double[3:4] == iota((ATOMS, 128), 0).astype(f32)).astype(f32)
            three, none = [query_hot] * 3, [jnp.zeros((3 * ATOMS, 128), f32)]
            rest = [jnp.zeros((128 - 6 * ATOMS, 128), f32)]
            spread = jnp.concatenate(
                [jnp.concatenate(three + none + rest, axis=0), jnp.concatenate(none + three + rest, axis=0)], axis=1
            )
            both = dot_nn(picks[tokens], spread.astype(bf16))
            scale = jnp.where(low, both[:HALF, :128], both[HALF:, :128])
            shift = jnp.where(low, both[:HALF, 128:], both[HALF:, 128:])
            r.argument[slot] = scale * distance + shift
            r.distance[slot] = distance
            for source, target in ((r.hops, r.hop_rows), (r.edges, r.edge_rows)):
                values = source[:, lanes].astype(f32)
                top, bottom = values[:HALF], values[HALF:]
                if s == 0:
                    target[slot] = jnp.where(low, top, half_swap(bottom))
                else:
                    target[slot] = jnp.where(low, half_swap(top), bottom)
            r.atom_rows[slot] = jnp.broadcast_to(double[3:4], (8, 128))


def table_grads(r, slots):
    lefts, rights = [], []
    for slot in range(slots):
        query_hot = (r.atom_rows[slot, 0:1, :] == iota((ATOMS, 128), 0).astype(f32)).astype(f32)
        keys = jnp.concatenate([query_hot[:, :HALF], query_hot[:, HALF:SLOT]], axis=0)
        keys = jnp.concatenate([keys, keys], axis=1).astype(bf16)
        values = jnp.concatenate([r.dargs[slot] * r.distance[slot], r.dargs[slot]], axis=1)
        both = dot_nn(keys, jnp.concatenate(bf16_parts(values, 2), axis=0))
        low = low_lanes(ATOMS)
        for index in range(2):
            lanes = slice(128 * index, 128 * (index + 1))
            rights.append(bf16_parts(jnp.where(low, both[:ATOMS, lanes], both[ATOMS:, lanes]), 2))
        lefts.append(query_hot.astype(bf16))
    left = jnp.concatenate(lefts, axis=1)
    right = jnp.concatenate(
        [jnp.concatenate([rights[2 * s + index][part] for s in range(slots)], axis=1) for index in range(2) for part in range(2)],
        axis=0,
    )
    result = dot_nt(left, right)
    return [
        result[:, 2 * ATOMS * index : 2 * ATOMS * index + ATOMS] + result[:, 2 * ATOMS * index + ATOMS : 2 * ATOMS * (index + 1)]
        for index in range(2)
    ]


def hold(tile, value):
    return value


def in_stages(stages, count, beside=lambda time: None):
    held = {}
    for time in range(count + len(stages) - 1):
        for k, stage in reversed(list(enumerate(stages))):
            if 0 <= time - k < count:
                held[time - k] = stage(time - k, held.get(time - k))
        beside(time)


TILES = PAIRS // TILE
ROWS = TILE // 128


def pair_forward(r, slot, beside=lambda time: None):
    bank = lax.rem(slot, 2)
    graph_on = r.flags[0, slot].astype(f32)
    space_on = r.flags[1, slot].astype(f32)
    factor = jnp.where(iota((H, 256), 1) < K, space_on, graph_on)
    r.lhs[...] = (r.base[...] * factor).astype(bf16)

    def kernels(tile, _):
        where = slice(tile * TILE, (tile + 1) * TILE)
        arg = four_rows(r.argument, slot, tile * ROWS)
        pieces = []
        for rows in strips():
            u = (arg - widen(r.cols[0, rows])) * widen(r.cols[1, rows])
            pieces.append(jnp.exp(widen(r.cols[2, rows]) - u * u).astype(bf16))
            r.left[bank, rows, where] = pieces[-1]
        return dot_halves(r.w1t[...], pieces)

    def hidden(tile, first):
        where = slice(tile * TILE, (tile + 1) * TILE)
        pieces = []
        for rows in strips():
            value, slope = gelu_pair(first[rows] + widen(r.cols[3, rows]))
            pieces.append(value)
            r.left[bank, slice(K + rows.start, K + rows.stop), where] = pieces[-1]
            r.slope[bank, rows, where] = slope
        hot = jnp.concatenate(
            [
                hot_rows(four_rows(r.hop_rows, slot, tile * ROWS), HOPS),
                hot_rows(four_rows(r.edge_rows, slot, tile * ROWS), HOT - HOPS),
            ],
            axis=0,
        ).astype(bf16)
        return dot_nn(r.lhs[:, : K + 2 * HOT], jnp.concatenate(pieces + [hot] * 2, axis=0))

    def biases(tile, bias):
        bias = bias.astype(bf16).astype(f32)
        for i in range(ROWS):
            r.bias[slot, pl.ds(tile * ROWS + i, H, stride=HALF), :] = bias[:, 128 * i : 128 * (i + 1)]

    in_stages([kernels, hold, hidden, hold, biases], TILES, beside)


def pair_backward(r, slot, between):
    bank = lax.rem(slot, 2)
    graph_on = r.flags[0, slot].astype(f32)
    space_on = r.flags[1, slot].astype(f32)
    twice(r.w2_twice, r.w2[:, :H] * space_on)

    def scores(tile, _):
        where = slice(tile * TILE, (tile + 1) * TILE)
        grad = jnp.concatenate(
            [r.bias[slot, pl.ds(tile * ROWS + i, H, stride=HALF), :] for i in range(ROWS)], axis=1
        )
        r.right[K:, where] = jnp.concatenate([grad * space_on, grad * graph_on], axis=0).astype(bf16)
        edge_hot = hot_rows(four_rows(r.edge_rows, slot, tile * ROWS), HOT - HOPS)
        edge_hot = jnp.where(iota((HOT - HOPS, TILE), 0) == EDGES, 1.0, edge_hot)
        r.left[bank, 2 * K :, where] = jnp.concatenate(
            [hot_rows(four_rows(r.hop_rows, slot, tile * ROWS), HOPS), edge_hot], axis=0
        ).astype(bf16)
        return dot_halves(r.w2_twice[...], [grad.astype(bf16)])

    def hidden(tile, d_second):
        where = slice(tile * TILE, (tile + 1) * TILE)
        pieces = []
        for rows in strips():
            pieces.append((d_second[rows] * r.slope[bank, rows, where].astype(f32)).astype(bf16))
            r.right[rows, where] = pieces[-1]
        return dot_halves(r.w1[...], pieces)

    def kernels(tile, d_gauss):
        where = slice(tile * TILE, (tile + 1) * TILE)
        arg = four_rows(r.argument, slot, tile * ROWS)
        d_arg = None
        for rows in strips():
            inv = widen(r.cols[4, rows])
            u = (arg - widen(r.cols[0, rows])) * inv
            q = d_gauss[rows] * r.left[bank, rows, where].astype(f32)
            w = q * u
            r.sums[0, rows] += fold_lanes(w)
            r.sums[1, rows] += fold_lanes(w * u - q)
            w = w * inv
            w = w[:8] + w[8:]
            d_arg = w if d_arg is None else d_arg + w
        d_arg = -jnp.sum(d_arg, axis=0, keepdims=True)
        for i in range(ROWS):
            at = tile * ROWS + i
            r.dargs[slot, at : at + 1, :] = d_arg[:, 128 * i : 128 * (i + 1)]

    in_stages([scores, hold, hidden, hold, kernels], TILES)
    between()
    r.acc_mixed[...] += dot_nt(r.left[bank], r.right[...])


def attend_group(r, s, first_slot, g):
    low = low_lanes(HALF)
    rows = span(s * SLOT, SLOT)
    if g == 0:
        r.work[0] = jnp.zeros((SLOT, D), f32)
    valid = iota((SLOT, GROUP * SLOT), 0) < r.lengths[first_slot + s]
    start, width, _ = window(g)
    q = r.joined[rows, start : start + width]
    k = r.joined[rows, D + start : D + start + width]
    v = r.joined[rows, 2 * D + start : 2 * D + start + width]
    scores = dot_nt(k, spread_heads(q, g)) * head_scale
    parts = []
    for pair in range(GROUP // 2):
        head = GROUP * g + 2 * pair
        one = r.bias[s, head * HALF : (head + 1) * HALF, :]
        two = r.bias[s, (head + 1) * HALF : (head + 2) * HALF, :]
        top = jnp.where(low, one, half_swap(two))
        bottom = jnp.where(low, half_swap(one), two)
        parts.append(jnp.concatenate([top, bottom], axis=0))
    scores = jnp.where(valid, scores + jnp.concatenate(parts, axis=1), neg_large)
    weights = jnp.exp(scores - jnp.max(scores, axis=0, keepdims=True))
    prob = (weights * (1.0 / jnp.sum(weights, axis=0, keepdims=True))).astype(bf16)
    r.prob[s, :, g * GROUP * SLOT : (g + 1) * GROUP * SLOT] = prob
    r.work[0, :, start : start + width] += gather_heads(dot_tn(prob, v), g)
    if g == GROUPS - 1:
        r.attended[rows, :] = r.work[0].astype(bf16)


def attend_back(r, s):
    low = low_lanes(HALF)
    rows = span(s * SLOT, SLOT)
    r.work[...] = jnp.zeros((3, SLOT, D), f32)
    for g in range(GROUPS):
        start, width, _ = window(g)
        lanes = slice(start, start + width)
        k = r.joined[rows, D + start : D + start + width]
        v = r.joined[rows, 2 * D + start : 2 * D + start + width]
        q_heads = spread_heads(r.joined[rows, lanes], g)
        d_heads = spread_heads(r.d_attended[rows, lanes], g)
        prob = r.prob[s, :, g * GROUP * SLOT : (g + 1) * GROUP * SLOT]
        wide = prob.astype(f32)
        d_prob = dot_nt(v, d_heads)
        inner = jnp.sum(wide * d_prob, axis=0, keepdims=True)
        d_scores = (wide * (d_prob - inner)).astype(bf16)
        r.work[0, :, lanes] += gather_heads(dot_tn(d_scores, k), g)
        r.work[1, :, lanes] += dot_nn(d_scores, q_heads)
        r.work[2, :, lanes] += dot_nn(prob, d_heads)
        d_wide = d_scores.astype(f32)
        for pair in range(GROUP // 2):
            head = GROUP * g + 2 * pair
            top = d_wide[:HALF, 128 * pair : 128 * (pair + 1)]
            bottom = d_wide[HALF:, 128 * pair : 128 * (pair + 1)]
            r.bias[s, head * HALF : (head + 1) * HALF, :] = jnp.where(low, top, half_swap(bottom))
            r.bias[s, (head + 1) * HALF : (head + 2) * HALF, :] = jnp.where(low, half_swap(top), bottom)
    r.joined[rows, 0:D] = (r.work[0] * head_scale).astype(bf16)
    r.joined[rows, D : 2 * D] = (r.work[1] * head_scale).astype(bf16)
    r.joined[rows, 2 * D : 3 * D] = r.work[2].astype(bf16)


def project(r, rows):
    scaled, _ = standardize(r.hidden[rows, :].astype(f32))
    normed = (scaled * row_of(r.attn_gain) + row_of(r.attn_shift)).astype(bf16)
    r.normed_a[rows, :] = normed
    for m in range(3):
        for t in range(2):
            at = m * D + t * HALF_D
            r.joined[rows, at : at + HALF_D] = dot_nn(normed, r.wqkv[t, m]).astype(bf16)


def feed(r, rows):
    halves = [slice(0, HALF_D), slice(HALF_D, D)]
    resid = r.hidden[rows, :].astype(f32)
    for t in range(2):
        resid = resid + dot_nn(r.attended[rows, halves[t]], r.wproj[t])
    scaled, inv_std = standardize(resid)
    normed = (scaled * row_of(r.ffn_gain) + row_of(r.ffn_shift)).astype(bf16)
    r.normed_f[rows, :] = normed
    pre = jnp.concatenate([dot_nn(normed, r.wup[t]) for t in range(2)], axis=1)
    value, slope = gelu_parts(pre + row_of(r.up_bias))
    active = value.astype(bf16)
    r.activated[rows, :] = active
    result = resid + row_of(r.down_bias)
    for t in range(2):
        result = result + dot_nn(active[:, halves[t]], r.wdown[t])
    r.out_rows[rows, :] = result.astype(bf16)
    cot = r.cotangent[rows, :]
    cot_wide = cot.astype(f32)
    d_active = jnp.concatenate([dot_nt(cot, r.wdown[t]) for t in range(2)], axis=1)
    d_hidden = (d_active * slope).astype(bf16)
    r.d_pre[rows, :] = d_hidden
    d_normed = dot_nt(d_hidden[:, halves[0]], r.wup[0]) + dot_nt(d_hidden[:, halves[1]], r.wup[1])
    d_resid = cot_wide + norm_back(d_normed, scaled, inv_std, row_of(r.ffn_gain))
    r.d_resid[rows, :] = d_resid
    branch = d_resid.astype(bf16)
    r.d_branch[rows, :] = branch
    for t in range(2):
        r.d_attended[rows, halves[t]] = dot_nt(branch, r.wproj[t]).astype(bf16)
    r.vectors[2:3, :] += column_sum(d_normed * scaled)
    r.vectors[3:4, :] += column_sum(d_normed)
    r.vectors[4:5, :] += column_sum(d_hidden.astype(f32))
    r.vectors[5:6, :] += column_sum(cot_wide)


def feed_grads(r, block):
    halves = [slice(0, HALF_D), slice(HALF_D, D)]
    if block == 0:
        grad = dot_tn(r.normed_f[...], r.d_pre[...]).astype(bf16)
        for t in range(2):
            r.fpart[t, :D, :] = grad[:, halves[t]]
        return
    left, right = (r.attended, r.d_branch) if block == 1 else (r.activated, r.cotangent)
    for t in range(2):
        grad = dot_tn(left[:, halves[t]], right[...]).astype(bf16)
        for side in range(2):
            r.fpart[t, D * block + HALF_D * side : D * block + HALF_D * (side + 1), :] = grad[:, halves[side]]


def qkv_grads(r, block):
    rows = slice(256 * block, 256 * (block + 1))
    for m in range(3):
        grad = dot_tn(r.normed_a[:, rows], r.joined[:, m * D : (m + 1) * D]).astype(bf16)
        for t in range(2):
            r.qpart[t, rows, m * HALF_D : (m + 1) * HALF_D] = grad[:, t * HALF_D : (t + 1) * HALF_D]


def finish_input(r, rows):
    d_normed = None
    for m in range(3):
        for t in range(2):
            at = m * D + t * HALF_D
            term = dot_nt(r.joined[rows, at : at + HALF_D], r.wqkv[t, m])
            d_normed = term if d_normed is None else d_normed + term
    scaled, inv_std = standardize(r.hidden[rows, :].astype(f32))
    grad = r.d_resid[rows, :] + norm_back(d_normed, scaled, inv_std, row_of(r.attn_gain))
    r.in_rows[rows, :] = grad.astype(bf16)
    r.vectors[0:1, :] += column_sum(d_normed * scaled)
    r.vectors[1:2, :] += column_sum(d_normed)


def pack_small(r, slots):
    tables = table_grads(r, slots)
    for v in range(6):
        for i in range(D // 128):
            at = VECTOR_ROWS + v * (D // 128) + i
            r.spart[at : at + 1, :] = r.vectors[v : v + 1, 128 * i : 128 * (i + 1)]
    r.spart[0:K, :] = r.acc_mixed[0:K, :K]
    r.spart[SECOND_ROWS : SECOND_ROWS + H, :] = square_turn(r.acc_mixed[K : 2 * K, K:])[:H]
    r.spart[TABLE_ROWS : TABLE_ROWS + H, :HOT] = square_turn(r.acc_mixed[2 * K :, K:])[H : 2 * H, :HOT]
    for index in range(2):
        rows = slice(TABLE_ROWS + ATOMS * index, TABLE_ROWS + ATOMS * (index + 1))
        r.spart[rows, HOT : HOT + ATOMS] = tables[index]
    ones = 2 * K + HOPS + EDGES
    r.spart[KERNEL_ROWS : KERNEL_ROWS + 1, :] = r.acc_mixed[ones : ones + 1, :K]
    for index in range(2):
        column = jnp.sum(r.sums[index] * r.cols[4], axis=1, keepdims=True)
        same = iota((K, K), 0) == iota((K, K), 1)
        at = KERNEL_ROWS + 1 + index
        r.spart[at : at + 1, :] = jnp.sum(jnp.where(same, column, 0.0), axis=0, keepdims=True)


class Stage:
    def __init__(self, names, near_inputs, carried, refs):
        self.r = SimpleNamespace(**dict(zip(names, refs)))
        r = self.r
        self.loads = {
            name: pltpu.make_async_copy(getattr(r, "given_" + name), getattr(r, name), r.input_sems.at[i])
            for i, name in enumerate(near_inputs)
        }
        self.stores = {
            name: pltpu.make_async_copy(getattr(r, name), getattr(r, name + "_far"), r.carry_sems.at[i])
            for i, name in enumerate(carried)
        }

    def load(self, *names):
        for name in names:
            self.loads[name].start()

    def need(self, *names):
        for name in names:
            self.loads[name].wait()

    def store(self, *names):
        for name in names:
            self.stores[name].start()

    def stored(self):
        for copy in self.stores.values():
            copy.wait()


def each_chunk(r, tokens, work):
    chunk = min(512, tokens)

    def one(c, _):
        work(r, span(c * chunk, chunk))
        return 0

    lax.fori_loop(0, tokens // chunk, one, 0)


def pair_moves(r, slot, back):
    bank = lax.rem(slot, 2)
    both = (r.left_far.at[slot], r.left.at[bank, : 2 * K]), (r.slope_far.at[slot], r.slope.at[bank])
    for index, (far, near) in enumerate(both):
        yield pltpu.make_async_copy(*((far, near) if back else (near, far)), r.pair_sems.at[bank, index])


def start_moves(r, slot, back):
    for copy in pair_moves(r, slot, back):
        copy.start()


def wait_moves(r, slot, back):
    for copy in pair_moves(r, slot, back):
        copy.wait()


def run(steps):
    for act, *where in steps:
        act(*where)


def at_time(index, plan):
    for k, steps in plan.items():
        pl.when(index == k)(functools.partial(run, steps))


FFN_BACK = {0: [(1, 1), (2, 1)], 3: [(0, 2)], 7: [(0, 3), (1, 2)]}
AFTER_GRADS = ([(0, 4), (1, 3), (2, 2)], [(0, 1), (1, 1), (2, 1)])
AFTER_HALF = ([(0, 5)], [])
AFTER_INPUT = ([(2, 3), (1, 4)], [(0, 2)])
FFN_PAIRS = {
    0: [(0, 6)], 2: [(2, 4)], 3: [(1, 5), (0, 7)], 5: [(2, 5)], 7: [(1, 6)], 9: [(2, 6)], 10: [(1, 7)], 12: [(2, 7)],
}
QKV_PAIRS = {
    2: [(0, 3)], 3: [(1, 2)], 6: [(1, 3), (2, 2), (0, 4)], 9: [(1, 4)], 10: [(0, 5)], 11: [(2, 3)], 12: [(1, 5)],
    13: [(0, 6)], 14: [(2, 4)], 15: [(1, 6)],
}


def layer_kernel(remote, names, near_inputs, carried, *refs):
    stage = Stage(names, near_inputs, carried, refs)
    r = stage.r
    stage.load(*[name for name in near_inputs if name not in ("hidden", "cotangent")])
    tokens = r.hidden.shape[0]
    slots = tokens // SLOT
    peers = Peers()
    if remote:
        greet(peers.everyone())
    whole = [r.wqkv, r.wup, r.wproj, r.wdown]
    given = [r.given_qkv, r.given_up, r.given_proj, r.given_down]
    targets = [w.at[peers.tp] for w in whole] if remote else whole
    loads = [
        pltpu.make_async_copy(src, dst, r.load_sems.at[i]) for i, (src, dst) in enumerate(zip(given, targets))
    ]
    for load in loads:
        load.start()
    stage.load("hidden", "cotangent")
    gather_plan = {}
    if remote:

        def whole_piece(index, tp):
            return whole[0].at[tp, index] if index < 3 else whole[index - 2].at[tp]

        gather = Gather(peers, whole_piece, r.gather_sends, r.gather_recvs)
        ffn = Reduction(peers, r.fpart, r.ftotal, r.f_core, r.f_tp, r.f_x, r.f_z, r.f_sends, r.f_recvs)
        qkv = Reduction(peers, r.qpart, r.qtotal, r.q_core, r.q_tp, r.q_x, r.q_z, r.q_sends, r.q_recvs)
        small = SmallReduction(peers, r.spart, r.stotal, r.s_near, r.s_z, r.s_sends, r.s_recvs)
        x, core = gather.onward_x, gather.onward_core
        gather_plan = {
            0: [(x, 0)], 1: [(x, 1)], 2: [(core, 0), (x, 2)], 3: [(core, 1), (x, 3), (core, 2)],
            4: [(x, 4)], 5: [(core, 3), (x, 5)], 6: [(core, 4)], 7: [(core, 5)],
        }

    def leave(which, block):
        near, far = ((r.ftotal, r.ftotal_far), (r.qtotal, r.qtotal_far))[which]
        rows = near.shape[0] // 3
        at = slice(block * rows, (block + 1) * rows)
        return pltpu.make_async_copy(near.at[at], far.at[at], r.leave_sems.at[3 * which + block])

    def advance(which, actions):
        if remote:
            for block, step in actions:
                (ffn, qkv)[which].act(block, step)
                if step == 7:
                    leave(which, block).start()

    def plan_of(*plans):
        times = sorted(set().union(*plans)) if remote else []
        return {
            k: [(advance, which, plan[k]) for which, plan in enumerate(plans) if k in plan] for k in times
        }

    stage.need(*[name for name in near_inputs if name not in ("hidden", "cotangent")])
    prepare_pairs(r)
    pair_tables(r, slots)
    if remote:
        await_greetings(peers.everyone())
        for load, indices in zip(loads, ((0, 1, 2), (3,), (4,), (5,))):
            load.wait()
            gather.start(indices)

    first_slot = peers.tp * slots
    alone = (5 * slots + 7) // 8

    def pairs(slot, _):
        pl.when(slot >= 2)(lambda: wait_moves(r, slot - 2, False))
        pair_forward(r, slot)
        start_moves(r, slot, False)
        at_time(slot, gather_plan)
        return 0

    def pairs_and_attention(slot, _):
        def beside(time):
            if 1 <= time <= GROUPS:
                attend_group(r, slot - alone, first_slot, time - 1)

        pl.when(slot >= 2)(lambda: wait_moves(r, slot - 2, False))
        pair_forward(r, slot, beside)
        start_moves(r, slot, False)
        at_time(slot, gather_plan)
        return 0

    def attend_one(s, _):
        for g in range(GROUPS):
            attend_group(r, s, first_slot, g)
        return 0

    lax.fori_loop(0, alone, pairs, 0)
    stage.need("hidden")
    if remote:
        for index in range(3):
            gather.arrive(index)
    else:
        for load in loads:
            load.wait()
    each_chunk(r, tokens, project)
    lax.fori_loop(alone, slots, pairs_and_attention, 0)
    lax.fori_loop(slots - alone, slots, attend_one, 0)
    stage.need("cotangent")
    if remote:
        for index in range(3, 6):
            gather.arrive(index)
    r.vectors[...] = jnp.zeros_like(r.vectors)
    each_chunk(r, tokens, feed)
    stage.store("out_rows")
    for slot in (slots - 2, slots - 1):
        wait_moves(r, slot, False)
    start_moves(r, 0, True)
    start_moves(r, 1, True)
    for block in range(3):
        feed_grads(r, block)
        advance(0, [(block, 0)])
    advance(0, [(0, 1)])

    back_plan, pair_plan = plan_of(FFN_BACK), plan_of(FFN_PAIRS, QKV_PAIRS)

    def back_one(s, _):
        attend_back(r, s)
        at_time(s, back_plan)
        return 0

    lax.fori_loop(0, slots, back_one, 0)
    for block in range(3):
        qkv_grads(r, block)
        advance(1, [(block, 0)])
    for which in range(2):
        advance(which, AFTER_GRADS[which])
    each_chunk(r, tokens, finish_input)
    stage.store("in_rows")
    for which in range(2):
        advance(which, AFTER_HALF[which] + AFTER_INPUT[which])
    for ref in (r.sums, r.acc_mixed, r.spart):
        ref[...] = jnp.zeros_like(ref)

    def pairs_back(slot, _):
        wait_moves(r, slot, True)
        pair_backward(r, slot, lambda: at_time(2 * slot, pair_plan))
        pl.when(slot + 2 < slots)(lambda: start_moves(r, slot + 2, True))
        at_time(2 * slot + 1, pair_plan)
        return 0

    lax.fori_loop(0, slots, pairs_back, 0)
    pack_small(r, slots)
    if remote:
        small.act(0)
        advance(1, [(2, 5), (0, 7)])
        small.act(1)
        advance(1, [(1, 7)])
        advance(1, [(2, 6)])
        small.act(2)
        advance(1, [(2, 7)])
        small.act(3)
        rows = pltpu.make_async_copy(r.stotal, r.stotal_far, r.leave_sems.at[6])
        rows.start()
        for which in range(2):
            advance(which, [(b, 8) for b in range(3)])
        small.act(4)
        gather.finish()
        for which in range(2):
            for block in range(3):
                leave(which, block).wait()
        rows.wait()
    else:
        stage.store("fpart", "qpart", "spart")
    stage.stored()


def call_stage(kernel, name, remote, collective, arrays, scalars, far, outs, carried, scratch):
    vm, sem = pltpu.VMEM, pltpu.SemaphoreType.DMA
    near = {n: vm(a.shape, a.dtype) for n, a in arrays.items() if n not in scalars + far}
    in_names = [n if n in scalars or n.endswith("_far") else "given_" + n for n in arrays]
    results = outs | {n + "_far": item for n, item in carried.items()}
    scratch = near | {n: vm(*item) for n, item in carried.items()} | scratch
    scratch |= {"input_sems": sem((len(near),)), "carry_sems": sem((len(carried),))}
    names = in_names + list(results) + list(scratch)
    values = pl.pallas_call(
        functools.partial(kernel, remote, names, list(near), list(carried)),
        in_specs=[pl.BlockSpec(memory_space=pltpu.SMEM if n in scalars else pl.ANY) for n in arrays],
        out_specs=[pl.BlockSpec(memory_space=pl.ANY)] * len(results),
        out_shape=[jax.ShapeDtypeStruct(*item) for item in results.values()],
        scratch_shapes=list(scratch.values()),
        compiler_params=pltpu.CompilerParams(
            vmem_limit_bytes=VMEM_BYTES, **(dict(collective_id=collective, has_side_effects=True) if remote else {})
        ),
        name=name,
    )(*arrays.values())
    return dict(zip(results, values))


def layer(remote, arrays):
    tokens = arrays["hidden"].shape[0]
    slots = tokens // SLOT
    v, sem = pltpu.VMEM, pltpu.SemaphoreType.DMA
    of_tokens = (tokens, D)
    table = (slots, HALF, 128)
    fshape, qshape, sshape = (3 * D, HALF_D), (D, 3 * HALF_D), (SMALL_ROWS, 128)
    outs = {"left_far": ((slots, 2 * K, PAIRS), bf16), "slope_far": ((slots, K, PAIRS), bf16)}
    carried = {"out_rows": (of_tokens, bf16), "in_rows": (of_tokens, bf16)}
    scratch = {
        "wqkv": v((2, 3, D, HALF_D), bf16), "wup": v((2, D, HALF_D), bf16), "wproj": v((2, HALF_D, D), bf16),
        "wdown": v((2, HALF_D, D), bf16), "load_sems": sem((4,)), "pair_sems": sem((2, 2)),
        "left": v((2, 2 * K + HOT, PAIRS), bf16), "slope": v((2, K, PAIRS), bf16),
        "right": v((K + 2 * H, PAIRS), bf16), "cols": v((5, K, 128), f32), "w1": v((2 * K, 2 * K), bf16), "w1t": v((2 * K, 2 * K), bf16),
        "w2": v((K, 128), f32), "w2_twice": v((2 * K, 2 * H), bf16), "base": v((H, 256), f32), "lhs": v((H, 256), bf16),
        "argument": v(table, f32), "distance": v(table, f32), "hop_rows": v(table, f32), "edge_rows": v(table, f32),
        "atom_rows": v((slots, 8, 128), f32), "dargs": v(table, f32), "bias": v((slots, H * HALF, 128), f32),
        "work": v((3, SLOT, D), f32), "normed_a": v(of_tokens, bf16), "joined": v((tokens, 3 * D), bf16),
        "prob": v((slots, SLOT, H * SLOT), bf16), "attended": v(of_tokens, bf16), "normed_f": v(of_tokens, bf16),
        "activated": v(of_tokens, bf16), "d_pre": v(of_tokens, bf16), "d_branch": v(of_tokens, bf16),
        "d_attended": v(of_tokens, bf16), "d_resid": v(of_tokens, f32), "vectors": v((8, D), f32),
        "sums": v((2, K, 128), f32), "acc_mixed": v((2 * K + HOT, K + 2 * H), f32),
    }
    parts = {"fpart": ((2,) + fshape, bf16), "qpart": ((2,) + qshape, bf16), "spart": (sshape, f32)}
    totals = {"ftotal": (fshape, bf16), "qtotal": (qshape, bf16), "stotal": (sshape, f32)}
    if remote:
        outs |= {n + "_far": item for n, item in totals.items()}
        scratch |= {n: v(*item) for n, item in (parts | totals).items()}
        scratch |= {"leave_sems": sem((7,)), "gather_sends": sem((6, 4)), "gather_recvs": sem((6, 4))}
        for name, shape in (("f", (D, HALF_D)), ("q", (D // 3, 3 * HALF_D))):
            keys = ("_core", "_tp", "_x", "_z", "_sends", "_recvs")
            scratch |= {name + key: item for key, item in zip(keys, big_scratch(*shape))}
        scratch |= dict(zip(("s_near", "s_z", "s_sends", "s_recvs"), small_scratch()))
    else:
        carried |= parts
    results = call_stage(
        layer_kernel, "layer", remote, 0, arrays, ("lengths", "flags"), ("qkv", "up", "proj", "down"), outs, carried,
        scratch,
    )
    sums = [results[n + "_far"] for n in (totals if remote else parts)]
    return results["out_rows_far"], results["in_rows_far"], sums


RESULTS = (
    "output", "grad_input", "attn_gain", "attn_shift", "qkv", "proj", "ffn_gain", "ffn_shift", "up", "up_bias", "down",
    "down_bias", "scale", "shift", "centers", "spreads", "first", "first_bias", "second", "hop", "edge",
)


def unpack_kernel(*refs):
    given = SimpleNamespace(**dict(zip(("out_rows", "in_rows", "fsum", "qsum", "rows"), refs)))
    far = SimpleNamespace(**dict(zip(RESULTS, refs[5:])))
    count = len(RESULTS)
    near = SimpleNamespace(**dict(zip(RESULTS, refs[5 + count : 5 + 2 * count])))
    fsum, qsum, rows, load_sems, store_sems = refs[5 + 2 * count :]
    moves = [(given.rows, rows)]
    sources = ((given.qsum, qsum, 3), (given.fsum, fsum, 9), (given.out_rows, near.output, 1), (given.in_rows, near.grad_input, 1))
    for src, dst, pieces in sources:
        height = src.shape[0] // pieces
        for i in range(pieces):
            at = slice(i * height, (i + 1) * height)
            moves.append((src.at[at], dst.at[at]))
    loads = [pltpu.make_async_copy(src, dst, load_sems.at[i]) for i, (src, dst) in enumerate(moves)]
    for load in loads:
        load.start()
    stores = []

    def store(src, dst):
        stores.append(pltpu.make_async_copy(src, dst, store_sems.at[len(stores)]))
        stores[-1].start()

    for i in range(3):
        loads[1 + i].wait()
        at = slice(256 * i, 256 * (i + 1))
        for m in range(3):
            near.qkv[m, at] = qsum[at, m * HALF_D : (m + 1) * HALF_D].astype(f32)
        store(near.qkv.at[:, at], far.qkv.at[:, at])
    for i in range(3):
        loads[4 + i].wait()
        at = slice(256 * i, 256 * (i + 1))
        near.up[at, :] = fsum[at, :].astype(f32)
        store(near.up.at[at], far.up.at[at])
    for block, name in ((1, "proj"), (2, "down")):
        for i in range(3):
            loads[4 + 3 * block + i].wait()
        ref = getattr(near, name)
        at = D * block
        ref[:, :HALF_D] = fsum[at : at + HALF_D, :].astype(f32)
        ref[:, HALF_D:] = fsum[at + HALF_D : at + D, :].astype(f32)
        store(ref, getattr(far, name))
    loads[13].wait()
    store(near.output, far.output)
    loads[14].wait()
    store(near.grad_input, far.grad_input)
    loads[0].wait()
    names = ("attn_gain", "attn_shift", "ffn_gain", "ffn_shift", "up_bias", "down_bias")
    for v, name in enumerate(names):
        for i in range(D // 128):
            getattr(near, name)[pl.ds(128 * i, 128)] = rows[VECTOR_ROWS + v * (D // 128) + i, :]
    near.first[...] = rows[0:K, :]
    near.second[...] = rows[SECOND_ROWS : SECOND_ROWS + H, :]
    table = rows[TABLE_ROWS : TABLE_ROWS + H, :]
    near.scale[...] = table[:ATOMS, HOT : HOT + ATOMS]
    near.shift[...] = table[ATOMS:, HOT : HOT + ATOMS]
    turned = square_turn(table)
    near.hop[...] = turned[:HOPS, :H]
    near.edge[...] = turned[HOPS : HOPS + EDGES, :H]
    lines = ("first_bias", "centers", "spreads")
    for i, name in enumerate(lines):
        getattr(near, name)[...] = rows[KERNEL_ROWS + i, :]
    for name in names + ("first", "second", "scale", "shift", "hop", "edge") + lines:
        store(getattr(near, name), getattr(far, name))
    for copy in stores:
        copy.wait()


def unpack(out_rows, in_rows, fsum, qsum, rows):
    tokens = out_rows.shape[0]
    vec, line, types = ((D,), f32), ((K,), f32), ((ATOMS, ATOMS), f32)
    shapes = (
        ((tokens, D), bf16), ((tokens, D), bf16), vec, vec, ((3, D, HALF_D), f32), ((HALF_D, D), f32), vec, vec,
        ((D, HALF_D), f32), vec, ((HALF_D, D), f32), vec, types, types, line, line, ((K, K), f32), line, ((H, K), f32),
        ((HOPS, H), f32), ((EDGES, H), f32),
    )
    anywhere = pl.BlockSpec(memory_space=pl.ANY)
    return pl.pallas_call(
        unpack_kernel,
        in_specs=[anywhere] * 5,
        out_specs=[anywhere] * len(shapes),
        out_shape=[jax.ShapeDtypeStruct(*item) for item in shapes],
        scratch_shapes=[pltpu.VMEM(*item) for item in shapes] + [
            pltpu.VMEM(fsum.shape, bf16), pltpu.VMEM(qsum.shape, bf16), pltpu.VMEM(rows.shape, f32),
            pltpu.SemaphoreType.DMA((15,)), pltpu.SemaphoreType.DMA((25,)),
        ],
        compiler_params=pltpu.CompilerParams(vmem_limit_bytes=VMEM_BYTES),
        name="unpack",
    )(out_rows, in_rows, fsum, qsum, rows)


def whole_weights(qkv_weight, up_weight, proj_weight, down_weight):
    columns = lambda w: jnp.stack(jnp.split(w, 2, axis=-1))
    rows = lambda w: jnp.stack(jnp.split(w, 2, axis=0))
    gather = lambda w, dim: lax.all_gather(w, "tp", axis=dim, tiled=True)
    return (
        columns(gather(qkv_weight.transpose(1, 0, 2), 2)), columns(gather(up_weight, 1)),
        rows(gather(proj_weight, 0)), rows(gather(down_weight, 0)),
    )


def sum_grads(fgrads, qgrads, small):
    total_f, total_q, rows = lax.psum((fgrads, qgrads, small), ("mol", "tp"))
    share = D // lax.axis_size("tp")
    at = lax.axis_index("tp") * share

    def columns(halves):
        return lax.dynamic_slice_in_dim(jnp.concatenate(list(halves), axis=-1), at, share, halves.ndim - 2)

    def rows_of(block):
        part = total_f[:, D * block : D * (block + 1)]
        sides = jnp.concatenate([part[:, :HALF_D], part[:, HALF_D:]], axis=2).reshape(D, D)
        return lax.dynamic_slice_in_dim(sides, at, share, 0)

    qkv = columns(total_q.reshape(2, D, 3, HALF_D)).transpose(1, 0, 2)
    return [v.astype(f32) for v in (qkv, columns(total_f[:, :D]), rows_of(1), rows_of(2))], rows


def body(
    mesh_shape,
    hidden_in, positions, atom_types, hop_counts, edge_types, lengths, branches,
    attn_gain, attn_shift, qkv_weight, proj_weight, ffn_gain, ffn_shift, up_weight, up_bias, down_weight, down_bias,
    kernel_scale, kernel_shift, centers, spreads, first_weight, first_bias, second_weight, hop_table, edge_table,
    cotangent,
):
    remote = mesh_shape["tp"] == 2 and mesh_shape["mol"] == 16 and branches.shape[0] == 8
    if remote:
        weights = (qkv_weight.transpose(1, 0, 2), up_weight, proj_weight, down_weight)
    else:
        weights = whole_weights(qkv_weight, up_weight, proj_weight, down_weight)
    arrays = dict(
        lengths=lengths, flags=branches.T, positions=positions, atoms=atom_types, hops=hop_counts.T,
        edges=edge_types.T, kernel_scale=kernel_scale, kernel_shift=kernel_shift, centers=centers, spreads=spreads,
        first_weight=first_weight, first_bias=first_bias, second_weight=second_weight.T, hop_table=hop_table,
        edge_table=edge_table, attn_gain=attn_gain, attn_shift=attn_shift, ffn_gain=ffn_gain, ffn_shift=ffn_shift,
        up_bias=up_bias, down_bias=down_bias, hidden=hidden_in, cotangent=cotangent,
        qkv=weights[0], up=weights[1], proj=weights[2], down=weights[3],
    )
    output, grad_input, sums = layer(remote, arrays)
    if remote:
        fsum, qsum, rows = sums
    else:
        big, rows = sum_grads(*sums)
        fsum, qsum = jnp.zeros((3 * D, HALF_D), bf16), jnp.zeros((D, 3 * HALF_D), bf16)
    output, grad_input, *grads = unpack(output, grad_input, fsum, qsum, rows)
    if not remote:
        grads[2], grads[6], grads[3], grads[8] = big
    grads[2] = grads[2].transpose(1, 0, 2)
    grads[16] = grads[16].T
    return (output, grad_input, *grads)


def solution(mesh):
    rows = P(("mol", "tp"), None)
    all_of = P()
    in_specs = (
        rows, P(None, ("mol", "tp")), P(("mol", "tp")), rows, rows, P("mol"), rows, all_of, all_of,
        P(None, None, "tp"), P("tp", None), all_of, all_of, P(None, "tp"), all_of, P("tp", None),
    ) + (all_of,) * 10 + (rows,)
    out_specs = (
        rows, rows, all_of, all_of, P(None, None, "tp"), P("tp", None), all_of, all_of, P(None, "tp"), all_of,
        P("tp", None),
    ) + (all_of,) * 10
    step = functools.partial(body, dict(mesh.shape))
    return jax.shard_map(step, mesh=mesh, in_specs=in_specs, out_specs=out_specs, check_vma=False)
```

profile of v0, /device:TPU:0, one launch (start us, length us, event | category | flops | bytes accessed | tf_op | source)
XLA Modules:
  0.0 143.7 jit_solution(4815096726793036146)
XLA Ops:
  0.7 137.8 %layer.1 = (bf16[8,256,4096]{2,1,0:T(8,128)(2,1)}, bf16[8,128,4096]{2,1,0:T(8,128)(2,1)}, bf16[2304,384]{1,0:T(8,128)(2,1)}, bf16[768,1152]{1,0:T(8,128)(2,1)}, ...) custom-call(s32[16]{0:T(128)} %refs_0_.1, s32[2,8]{1,0:T(2,128)} %bitcast.11, ...), custom_call_target="tpu_custom_call" | custom-call | tf_op jit(solution)/shard_map/layer/pallas_call | solution.py:1084
  138.5 5.0 %unpack.1 = (bf16[512,768]{1,0:T(8,128)(2,1)}, bf16[512,768]{1,0:T(8,128)(2,1)}, f32[768]{0:T(1024)}, f32[768]{0:T(1024)}, f32[3,768,384]{2,1,0:T(8,128)}, /*ind...) custom-call(bf16[512,768]{1,0:T(8,128)(2,1)} %get-tuple-element.47.r, ...), custom_call_target="tpu_custom_call" | custom-call | tf_op jit(solution)/shard_map/unpack/pallas_call | solution.py:1223
where the time goes:
time: 144 us
  Pallas kernels  143 us (99%)
    pallas_call x1, Pallas kernels, call_stage(): pl.pallas_call(functools.partial(kernel, remote, names, list(near), list(...  138 us
    pallas_call x1, Pallas kernels, unpack(): pl.pallas_call(unpack_kernel, in_specs=[anywhere] * 5, out_specs=[anywher...  4.97 us

commit v1 on v0

--- a/solution.py
+++ b/solution.py
@@ -559,20 +559,29 @@
     return value
 
 
-def in_stages(stages, count, beside=lambda time: None):
+def staged(stages, count):
     held = {}
-    for time in range(count + len(stages) - 1):
+
+    def step(time):
         for k, stage in reversed(list(enumerate(stages))):
             if 0 <= time - k < count:
                 held[time - k] = stage(time - k, held.get(time - k))
-        beside(time)
+
+    return [functools.partial(step, time) for time in range(count + len(stages) - 1)]
+
+
+def run_beside(*step_lists):
+    for time in range(max(map(len, step_lists))):
+        for steps in step_lists:
+            if time < len(steps):
+                steps[time]()
 
 
 TILES = PAIRS // TILE
 ROWS = TILE // 128
 
 
-def pair_forward(r, slot, beside=lambda time: None):
+def pair_forward(r, slot, beside=()):
     bank = lax.rem(slot, 2)
     graph_on = r.flags[0, slot].astype(f32)
     space_on = r.flags[1, slot].astype(f32)
@@ -611,7 +620,7 @@
         for i in range(ROWS):
             r.bias[slot, pl.ds(tile * ROWS + i, H, stride=HALF), :] = bias[:, 128 * i : 128 * (i + 1)]
 
-    in_stages([kernels, hold, hidden, hold, biases], TILES, beside)
+    run_beside(staged([kernels, hold, hidden, hold, biases], TILES), beside)
 
 
 def pair_backward(r, slot, between):
@@ -660,58 +669,68 @@
             at = tile * ROWS + i
             r.dargs[slot, at : at + 1, :] = d_arg[:, 128 * i : 128 * (i + 1)]
 
-    in_stages([scores, hold, hidden, hold, kernels], TILES)
+    run_beside(staged([scores, hold, hidden, hold, kernels], TILES))
     between()
     r.acc_mixed[...] += dot_nt(r.left[bank], r.right[...])
 
 
-def attend_group(r, s, first_slot, g):
+def attend_steps(r, s, first_slot):
     low = low_lanes(HALF)
     rows = span(s * SLOT, SLOT)
-    if g == 0:
-        r.work[0] = jnp.zeros((SLOT, D), f32)
-    valid = iota((SLOT, GROUP * SLOT), 0) < r.lengths[first_slot + s]
-    start, width, _ = window(g)
-    q = r.joined[rows, start : start + width]
-    k = r.joined[rows, D + start : D + start + width]
-    v = r.joined[rows, 2 * D + start : 2 * D + start + width]
-    scores = dot_nt(k, spread_heads(q, g)) * head_scale
-    parts = []
-    for pair in range(GROUP // 2):
-        head = GROUP * g + 2 * pair
-        one = r.bias[s, head * HALF : (head + 1) * HALF, :]
-        two = r.bias[s, (head + 1) * HALF : (head + 2) * HALF, :]
-        top = jnp.where(low, one, half_swap(two))
-        bottom = jnp.where(low, half_swap(one), two)
-        parts.append(jnp.concatenate([top, bottom], axis=0))
-    scores = jnp.where(valid, scores + jnp.concatenate(parts, axis=1), neg_large)
-    weights = jnp.exp(scores - jnp.max(scores, axis=0, keepdims=True))
-    prob = (weights * (1.0 / jnp.sum(weights, axis=0, keepdims=True))).astype(bf16)
-    r.prob[s, :, g * GROUP * SLOT : (g + 1) * GROUP * SLOT] = prob
-    r.work[0, :, start : start + width] += gather_heads(dot_tn(prob, v), g)
-    if g == GROUPS - 1:
-        r.attended[rows, :] = r.work[0].astype(bf16)
+
+    def scores(g, _):
+        if g == 0:
+            r.work[0] = jnp.zeros((SLOT, D), f32)
+        start, width, _ = window(g)
+        q = r.joined[rows, start : start + width]
+        return dot_nt(r.joined[rows, D + start : D + start + width], spread_heads(q, g))
+
+    def mix(g, products):
+        start, width, _ = window(g)
+        valid = iota((SLOT, GROUP * SLOT), 0) < r.lengths[first_slot + s]
+        parts = []
+        for pair in range(GROUP // 2):
+            head = GROUP * g + 2 * pair
+            one = r.bias[s, head * HALF : (head + 1) * HALF, :]
+            two = r.bias[s, (head + 1) * HALF : (head + 2) * HALF, :]
+            top = jnp.where(low, one, half_swap(two))
+            bottom = jnp.where(low, half_swap(one), two)
+            parts.append(jnp.concatenate([top, bottom], axis=0))
+        values = jnp.where(valid, products * head_scale + jnp.concatenate(parts, axis=1), neg_large)
+        weights = jnp.exp(values - jnp.max(values, axis=0, keepdims=True))
+        prob = (weights * (1.0 / jnp.sum(weights, axis=0, keepdims=True))).astype(bf16)
+        r.prob[s, :, g * GROUP * SLOT : (g + 1) * GROUP * SLOT] = prob
+        return dot_tn(prob, r.joined[rows, 2 * D + start : 2 * D + start + width])
+
+    def gather(g, mixed):
+        start, width, _ = window(g)
+        r.work[0, :, start : start + width] += gather_heads(mixed, g)
+        if g == GROUPS - 1:
+            r.attended[rows, :] = r.work[0].astype(bf16)
+
+    return staged([scores, hold, mix, hold, gather], GROUPS)
 
 
 def attend_back(r, s):
     low = low_lanes(HALF)
     rows = span(s * SLOT, SLOT)
     r.work[...] = jnp.zeros((3, SLOT, D), f32)
-    for g in range(GROUPS):
+
+    def lanes_of(g):
         start, width, _ = window(g)
-        lanes = slice(start, start + width)
-        k = r.joined[rows, D + start : D + start + width]
-        v = r.joined[rows, 2 * D + start : 2 * D + start + width]
-        q_heads = spread_heads(r.joined[rows, lanes], g)
-        d_heads = spread_heads(r.d_attended[rows, lanes], g)
+        return slice(start, start + width)
+
+    def probabilities(g, _):
+        lanes = lanes_of(g)
+        v = r.joined[rows, 2 * D + lanes.start : 2 * D + lanes.stop]
+        return dot_nt(v, spread_heads(r.d_attended[rows, lanes], g))
+
+    def scores(g, d_prob):
+        lanes = lanes_of(g)
         prob = r.prob[s, :, g * GROUP * SLOT : (g + 1) * GROUP * SLOT]
         wide = prob.astype(f32)
-        d_prob = dot_nt(v, d_heads)
         inner = jnp.sum(wide * d_prob, axis=0, keepdims=True)
         d_scores = (wide * (d_prob - inner)).astype(bf16)
-        r.work[0, :, lanes] += gather_heads(dot_tn(d_scores, k), g)
-        r.work[1, :, lanes] += dot_nn(d_scores, q_heads)
-        r.work[2, :, lanes] += dot_nn(prob, d_heads)
         d_wide = d_scores.astype(f32)
         for pair in range(GROUP // 2):
             head = GROUP * g + 2 * pair
@@ -719,6 +738,19 @@
             bottom = d_wide[HALF:, 128 * pair : 128 * (pair + 1)]
             r.bias[s, head * HALF : (head + 1) * HALF, :] = jnp.where(low, top, half_swap(bottom))
             r.bias[s, (head + 1) * HALF : (head + 2) * HALF, :] = jnp.where(low, half_swap(top), bottom)
+        return (
+            dot_tn(d_scores, r.joined[rows, D + lanes.start : D + lanes.stop]),
+            dot_nn(d_scores, spread_heads(r.joined[rows, lanes], g)),
+            dot_nn(prob, spread_heads(r.d_attended[rows, lanes], g)),
+        )
+
+    def gather(g, products):
+        lanes = lanes_of(g)
+        r.work[0, :, lanes] += gather_heads(products[0], g)
+        r.work[1, :, lanes] += products[1]
+        r.work[2, :, lanes] += products[2]
+
+    run_beside(staged([probabilities, hold, scores, hold, gather], GROUPS))
     r.joined[rows, 0:D] = (r.work[0] * head_scale).astype(bf16)
     r.joined[rows, D : 2 * D] = (r.work[1] * head_scale).astype(bf16)
     r.joined[rows, 2 * D : 3 * D] = r.work[2].astype(bf16)
@@ -978,19 +1010,14 @@
         return 0
 
     def pairs_and_attention(slot, _):
-        def beside(time):
-            if 1 <= time <= GROUPS:
-                attend_group(r, slot - alone, first_slot, time - 1)
-
         pl.when(slot >= 2)(lambda: wait_moves(r, slot - 2, False))
-        pair_forward(r, slot, beside)
+        pair_forward(r, slot, attend_steps(r, slot - alone, first_slot))
         start_moves(r, slot, False)
         at_time(slot, gather_plan)
         return 0
 
     def attend_one(s, _):
-        for g in range(GROUPS):
-            attend_group(r, s, first_slot, g)
+        run_beside(attend_steps(r, s, first_slot))
         return 0
 
     lax.fori_loop(0, alone, pairs, 0)

time: 144 us -> 138 us (0.958)
  Pallas kernels: 143 us -> 137 us
    pallas_call x1, Pallas kernels: 138 us -> 132 us  [call_stage(): pl.pallas_call(functools.partial(kernel, remote, names, list(near), list(...]
where the time goes in v1:
time: 138 us
  Pallas kernels  137 us (99%)
    pallas_call x1, Pallas kernels, call_stage(): pl.pallas_call(functools.partial(kernel, remote, names, list(near), list(...  132 us
    pallas_call x1, Pallas kernels, unpack(): pl.pallas_call(unpack_kernel, in_specs=[anywhere] * 5, out_specs=[anywher...  4.97 us

profile of v1, /device:TPU:0, one launch (start us, length us, event | category | flops | bytes accessed | tf_op | source)
XLA Modules:
  0.0 138.0 jit_solution(15129459119203073955)
XLA Ops:
  0.7 132.2 %layer.1 = (bf16[8,256,4096]{2,1,0:T(8,128)(2,1)}, bf16[8,128,4096]{2,1,0:T(8,128)(2,1)}, bf16[2304,384]{1,0:T(8,128)(2,1)}, bf16[768,1152]{1,0:T(8,128)(2,1)}, ...) custom-call(s32[16]{0:T(128)} %refs_0_.1, s32[2,8]{1,0:T(2,128)} %bitcast.11, ...), custom_call_target="tpu_custom_call" | custom-call | tf_op jit(solution)/shard_map/layer/pallas_call | solution.py:1111
  132.8 5.0 %unpack.1 = (bf16[512,768]{1,0:T(8,128)(2,1)}, bf16[512,768]{1,0:T(8,128)(2,1)}, f32[768]{0:T(1024)}, f32[768]{0:T(1024)}, f32[3,768,384]{2,1,0:T(8,128)}, /*ind...) custom-call(bf16[512,768]{1,0:T(8,128)(2,1)} %get-tuple-element.47.r, ...), custom_call_target="tpu_custom_call" | custom-call | tf_op jit(solution)/shard_map/unpack/pallas_call | solution.py:1250

commit v2 on v1

--- a/solution.py
+++ b/solution.py
@@ -623,7 +623,7 @@
     run_beside(staged([kernels, hold, hidden, hold, biases], TILES), beside)
 
 
-def pair_backward(r, slot, between):
+def pair_backward(r, slot):
     bank = lax.rem(slot, 2)
     graph_on = r.flags[0, slot].astype(f32)
     space_on = r.flags[1, slot].astype(f32)
@@ -669,9 +669,16 @@
             at = tile * ROWS + i
             r.dargs[slot, at : at + 1, :] = d_arg[:, 128 * i : 128 * (i + 1)]
 
-    run_beside(staged([scores, hold, hidden, hold, kernels], TILES))
-    between()
-    r.acc_mixed[...] += dot_nt(r.left[bank], r.right[...])
+    def products(tile, _):
+        if tile % 2 == 1:
+            where = slice((tile - 1) * TILE, (tile + 1) * TILE)
+            return dot_nt(r.left[bank, :, where], r.right[:, where])
+
+    def add_products(tile, values):
+        if tile % 2 == 1:
+            r.acc_mixed[...] += values
+
+    run_beside(staged([scores, hold, hidden, hold, kernels, products, hold, add_products], TILES))
 
 
 def attend_steps(r, s, first_slot):
@@ -1069,7 +1076,8 @@
 
     def pairs_back(slot, _):
         wait_moves(r, slot, True)
-        pair_backward(r, slot, lambda: at_time(2 * slot, pair_plan))
+        pair_backward(r, slot)
+        at_time(2 * slot, pair_plan)
         pl.when(slot + 2 < slots)(lambda: start_moves(r, slot + 2, True))
         at_time(2 * slot + 1, pair_plan)
         return 0

time: 138 us -> 137 us (level)
  no operation moved by 1% of the time
where the time goes in v2:
time: 137 us
  Pallas kernels  136 us (99%)
    pallas_call x1, Pallas kernels, call_stage(): pl.pallas_call(functools.partial(kernel, remote, names, list(near), list(...  131 us
    pallas_call x1, Pallas kernels, unpack(): pl.pallas_call(unpack_kernel, in_specs=[anywhere] * 5, out_specs=[anywher...  4.97 us

profile of v2, /device:TPU:0, one launch (start us, length us, event | category | flops | bytes accessed | tf_op | source)
XLA Modules:
  0.0 137.2 jit_solution(5509552512860027087)
XLA Ops:
  0.7 131.4 %layer.1 = (bf16[8,256,4096]{2,1,0:T(8,128)(2,1)}, bf16[8,128,4096]{2,1,0:T(8,128)(2,1)}, bf16[2304,384]{1,0:T(8,128)(2,1)}, bf16[768,1152]{1,0:T(8,128)(2,1)}, ...) custom-call(s32[16]{0:T(128)} %refs_0_.1, s32[2,8]{1,0:T(2,128)} %bitcast.11, ...), custom_call_target="tpu_custom_call" | custom-call | tf_op jit(solution)/shard_map/layer/pallas_call | solution.py:1119
  132.1 5.0 %unpack.1 = (bf16[512,768]{1,0:T(8,128)(2,1)}, bf16[512,768]{1,0:T(8,128)(2,1)}, f32[768]{0:T(1024)}, f32[768]{0:T(1024)}, f32[3,768,384]{2,1,0:T(8,128)}, /*ind...) custom-call(bf16[512,768]{1,0:T(8,128)(2,1)} %get-tuple-element.47.r, ...), custom_call_target="tpu_custom_call" | custom-call | tf_op jit(solution)/shard_map/unpack/pallas_call | solution.py:1258

commit v3 on v2

--- a/solution.py
+++ b/solution.py
@@ -681,13 +681,13 @@
     run_beside(staged([scores, hold, hidden, hold, kernels, products, hold, add_products], TILES))
 
 
-def attend_steps(r, s, first_slot):
+def attend_steps(r, s, first_slot, side=0):
     low = low_lanes(HALF)
     rows = span(s * SLOT, SLOT)
 
     def scores(g, _):
         if g == 0:
-            r.work[0] = jnp.zeros((SLOT, D), f32)
+            r.work[3 * side] = jnp.zeros((SLOT, D), f32)
         start, width, _ = window(g)
         q = r.joined[rows, start : start + width]
         return dot_nt(r.joined[rows, D + start : D + start + width], spread_heads(q, g))
@@ -711,17 +711,16 @@
 
     def gather(g, mixed):
         start, width, _ = window(g)
-        r.work[0, :, start : start + width] += gather_heads(mixed, g)
+        r.work[3 * side, :, start : start + width] += gather_heads(mixed, g)
         if g == GROUPS - 1:
-            r.attended[rows, :] = r.work[0].astype(bf16)
+            r.attended[rows, :] = r.work[3 * side].astype(bf16)
 
     return staged([scores, hold, mix, hold, gather], GROUPS)
 
 
-def attend_back(r, s):
+def attend_back_steps(r, s, side):
     low = low_lanes(HALF)
     rows = span(s * SLOT, SLOT)
-    r.work[...] = jnp.zeros((3, SLOT, D), f32)
 
     def lanes_of(g):
         start, width, _ = window(g)
@@ -729,6 +728,9 @@
 
     def probabilities(g, _):
         lanes = lanes_of(g)
+        if g == 0:
+            for i in range(3):
+                r.work[3 * side + i] = jnp.zeros((SLOT, D), f32)
         v = r.joined[rows, 2 * D + lanes.start : 2 * D + lanes.stop]
         return dot_nt(v, spread_heads(r.d_attended[rows, lanes], g))
 
@@ -753,14 +755,15 @@
 
     def gather(g, products):
         lanes = lanes_of(g)
-        r.work[0, :, lanes] += gather_heads(products[0], g)
-        r.work[1, :, lanes] += products[1]
-        r.work[2, :, lanes] += products[2]
-
-    run_beside(staged([probabilities, hold, scores, hold, gather], GROUPS))
-    r.joined[rows, 0:D] = (r.work[0] * head_scale).astype(bf16)
-    r.joined[rows, D : 2 * D] = (r.work[1] * head_scale).astype(bf16)
-    r.joined[rows, 2 * D : 3 * D] = r.work[2].astype(bf16)
+        r.work[3 * side, :, lanes] += gather_heads(products[0], g)
+        r.work[3 * side + 1, :, lanes] += products[1]
+        r.work[3 * side + 2, :, lanes] += products[2]
+        if g == GROUPS - 1:
+            r.joined[rows, 0:D] = (r.work[3 * side] * head_scale).astype(bf16)
+            r.joined[rows, D : 2 * D] = (r.work[3 * side + 1] * head_scale).astype(bf16)
+            r.joined[rows, 2 * D : 3 * D] = r.work[3 * side + 2].astype(bf16)
+
+    return staged([probabilities, hold, scores, hold, gather], GROUPS)
 
 
 def project(r, rows):
@@ -1023,8 +1026,9 @@
         at_time(slot, gather_plan)
         return 0
 
-    def attend_one(s, _):
-        run_beside(attend_steps(r, s, first_slot))
+    def attend_two(i, _):
+        s = slots - alone + 2 * i
+        run_beside(attend_steps(r, s, first_slot, 0), attend_steps(r, s + 1, first_slot, 1))
         return 0
 
     lax.fori_loop(0, alone, pairs, 0)
@@ -1037,7 +1041,9 @@
             load.wait()
     each_chunk(r, tokens, project)
     lax.fori_loop(alone, slots, pairs_and_attention, 0)
-    lax.fori_loop(slots - alone, slots, attend_one, 0)
+    lax.fori_loop(0, alone // 2, attend_two, 0)
+    if alone % 2 == 1:
+        run_beside(attend_steps(r, slots - 1, first_slot))
     stage.need("cotangent")
     if remote:
         for index in range(3, 6):
@@ -1056,12 +1062,13 @@
 
     back_plan, pair_plan = plan_of(FFN_BACK), plan_of(FFN_PAIRS, QKV_PAIRS)
 
-    def back_one(s, _):
-        attend_back(r, s)
-        at_time(s, back_plan)
+    def back_two(i, _):
+        run_beside(attend_back_steps(r, 2 * i, 0), attend_back_steps(r, 2 * i + 1, 1))
+        at_time(2 * i, back_plan)
+        at_time(2 * i + 1, back_plan)
         return 0
 
-    lax.fori_loop(0, slots, back_one, 0)
+    lax.fori_loop(0, slots // 2, back_two, 0)
     for block in range(3):
         qkv_grads(r, block)
         advance(1, [(block, 0)])
@@ -1147,7 +1154,7 @@
         "w2": v((K, 128), f32), "w2_twice": v((2 * K, 2 * H), bf16), "base": v((H, 256), f32), "lhs": v((H, 256), bf16),
         "argument": v(table, f32), "distance": v(table, f32), "hop_rows": v(table, f32), "edge_rows": v(table, f32),
         "atom_rows": v((slots, 8, 128), f32), "dargs": v(table, f32), "bias": v((slots, H * HALF, 128), f32),
-        "work": v((3, SLOT, D), f32), "normed_a": v(of_tokens, bf16), "joined": v((tokens, 3 * D), bf16),
+        "work": v((6, SLOT, D), f32), "normed_a": v(of_tokens, bf16), "joined": v((tokens, 3 * D), bf16),
         "prob": v((slots, SLOT, H * SLOT), bf16), "attended": v(of_tokens, bf16), "normed_f": v(of_tokens, bf16),
         "activated": v(of_tokens, bf16), "d_pre": v(of_tokens, bf16), "d_branch": v(of_tokens, bf16),
         "d_attended": v(of_tokens, bf16), "d_resid": v(of_tokens, f32), "vectors": v((8, D), f32),

time: 137 us -> 135 us (0.985)
  Pallas kernels: 136 us -> 134 us
    pallas_call x1, Pallas kernels: 131 us -> 129 us  [call_stage(): pl.pallas_call(functools.partial(kernel, remote, names, list(near), list(...]
where the time goes in v3:
time: 135 us
  Pallas kernels  134 us (99%)
    pallas_call x1, Pallas kernels, call_stage(): pl.pallas_call(functools.partial(kernel, remote, names, list(near), list(...  129 us
    pallas_call x1, Pallas kernels, unpack(): pl.pallas_call(unpack_kernel, in_specs=[anywhere] * 5, out_specs=[anywher...  4.97 us

profile of v3, /device:TPU:0, one launch (start us, length us, event | category | flops | bytes accessed | tf_op | source)
XLA Modules:
  0.0 135.0 jit_solution(7012021380611915402)
XLA Ops:
  0.7 129.1 %layer.1 = (bf16[8,256,4096]{2,1,0:T(8,128)(2,1)}, bf16[8,128,4096]{2,1,0:T(8,128)(2,1)}, bf16[2304,384]{1,0:T(8,128)(2,1)}, bf16[768,1152]{1,0:T(8,128)(2,1)}, ...) custom-call(s32[16]{0:T(128)} %refs_0_.1, s32[2,8]{1,0:T(2,128)} %bitcast.11, ...), custom_call_target="tpu_custom_call" | custom-call | tf_op jit(solution)/shard_map/layer/pallas_call | solution.py:1126
  129.8 5.0 %unpack.1 = (bf16[512,768]{1,0:T(8,128)(2,1)}, bf16[512,768]{1,0:T(8,128)(2,1)}, f32[768]{0:T(1024)}, f32[768]{0:T(1024)}, f32[3,768,384]{2,1,0:T(8,128)}, /*ind...) custom-call(bf16[512,768]{1,0:T(8,128)(2,1)} %get-tuple-element.47.r, ...), custom_call_target="tpu_custom_call" | custom-call | tf_op jit(solution)/shard_map/unpack/pallas_call | solution.py:1265
